TPU v7x, 512 devices: a whole 4x8x8 slice. The times are simulated.
512 devices in a mesh: dp: 8 (over z_hi, core), pipe: 8 (over z_lo, x), tensor: 8 (over y).
Axes of the slice: x: 4, y: 8, z: 8 (z_hi: 4, z_lo: 2; z = z_hi * 2 + z_lo), core: 2. Of those that a mesh axis runs over, the one named last changes fastest.
Arguments:
- normed: bfloat16 [8, 1024, 8192], P('pipe', 'tensor', 'dp'), may hold values from -6 to 6
- w_query: bfloat16 [8, 8192, 4096], P('pipe', 'dp', 'tensor'), may hold values from -0.0625 to 0.0625
- neighbour_kv: bfloat16 [8, 8, 8, 2, 128, 4096], P('dp', None, 'pipe', None, None, 'tensor'), may hold values from -190 to 190
- counts: int32 [8, 8, 2], P('pipe', 'dp'), may hold values from 1 to 4
- w_out: bfloat16 [8, 4096, 8192], P('pipe', 'tensor', 'dp'), may hold values from -0.75 to 0.75
Outputs:
- mixed: bfloat16 [8, 1024, 8192], P('pipe', 'tensor', 'dp')
All inputs are finite; a program needn't handle non-finite values.
Results may differ from a plain program's by a relative error of at most 0.025.
Values may be sent and summed in bfloat16 or wider, within the bound.
A program may use at most 64 MiB of HBM per device.

v0:
```python
import math

import jax
import jax.numpy as jnp
from jax import lax
from jax.sharding import PartitionSpec as P

HEADS = 32
SLOTS = 4


def attend_blocks(queries, neighbours, head_count):
    block_count, row_count, feature_width = queries.shape
    head_size = feature_width // head_count
    key_length = neighbours.shape[2]
    query_heads = queries.reshape(block_count, row_count, head_count, head_size)
    key_heads = neighbours[:, 0].reshape(block_count, key_length, head_count, head_size)
    value_heads = neighbours[:, 1].reshape(block_count, key_length, head_count, head_size)
    scores = jnp.einsum(
        "bihd,bjhd->bhij", query_heads, key_heads, preferred_element_type=jnp.float32
    ) * (1.0 / math.sqrt(head_size))
    block_max = jnp.max(scores, axis=3)
    exponent = jnp.exp(scores - block_max[..., None])
    block_sum = jnp.sum(exponent, axis=3)
    weights = exponent.astype(jnp.bfloat16)
    block_out = jnp.einsum(
        "bhij,bjhd->bihd", weights, value_heads, preferred_element_type=jnp.float32
    )
    return (block_max, block_sum, block_out.reshape(block_count, row_count, feature_width))


def combine_slots(block_max, block_sum, block_out, count_row, slot_count, head_count):
    span_count = count_row.shape[0]
    row_count = block_out.shape[1]
    feature_width = block_out.shape[2]
    head_size = feature_width // head_count
    slot_valid = jnp.arange(slot_count, dtype=jnp.int32)[None, :] < count_row[:, None]
    mask_full = slot_valid[:, :, None, None]
    block_max = block_max.reshape(span_count, slot_count, head_count, row_count)
    block_sum = block_sum.reshape(span_count, slot_count, head_count, row_count)
    span_max = jnp.max(jnp.where(mask_full, block_max, -jnp.inf), axis=1)
    factor = jnp.where(mask_full, jnp.exp(block_max - span_max[:, None]), 0.0)
    denominator = jnp.sum(factor * block_sum, axis=1)
    pieces = block_out.reshape(span_count, slot_count, row_count, head_count, head_size)
    factor_rows = jnp.transpose(factor, (0, 1, 3, 2))[..., None]
    numerator = jnp.sum(factor_rows * pieces, axis=1)
    result = numerator / jnp.transpose(denominator, (0, 2, 1))[..., None]
    return result.reshape(span_count * row_count, feature_width).astype(jnp.bfloat16)


def on_device(normed, w_query, neighbour_kv, counts, w_out):
    head_count = HEADS // lax.axis_size("tensor")
    partial_query = jnp.dot(
        lax.all_gather(normed[0], "tensor", axis=0, tiled=True),
        w_query[0],
        preferred_element_type=jnp.float32,
    )
    queries = lax.psum_scatter(partial_query, "dp", scatter_dimension=0, tiled=True).astype(
        jnp.bfloat16
    )
    count_row = counts[0, 0]
    span_count = count_row.shape[0]
    row_count = queries.shape[0] // span_count
    feature_width = queries.shape[1]
    key_length = neighbour_kv.shape[4]
    span_queries = queries.reshape(span_count, 1, row_count, feature_width)
    block_queries = jnp.broadcast_to(span_queries, (span_count, SLOTS, row_count, feature_width))
    received = lax.all_to_all(
        lax.all_to_all(neighbour_kv, "dp", split_axis=1, concat_axis=0, tiled=True),
        "pipe",
        split_axis=0,
        concat_axis=2,
        tiled=True,
    )
    neighbours = received.reshape(span_count * SLOTS, 2, key_length, feature_width)
    flat_queries = block_queries.reshape(span_count * SLOTS, row_count, feature_width)
    block_max, block_sum, block_out = attend_blocks(flat_queries, neighbours, head_count)
    attended = combine_slots(block_max, block_sum, block_out, count_row, SLOTS, head_count)
    partial_mixed = jnp.dot(
        lax.all_gather(attended, "dp", axis=0, tiled=True),
        w_out[0],
        preferred_element_type=jnp.float32,
    )
    mixed = lax.psum_scatter(
        partial_mixed.astype(jnp.bfloat16), "tensor", scatter_dimension=0, tiled=True
    )
    return mixed[None]


def solution(mesh):
    return jax.shard_map(
        on_device,
        mesh=mesh,
        in_specs=(
            P("pipe", "tensor", "dp"),
            P("pipe", "dp", "tensor"),
            P("dp", None, "pipe", None, None, "tensor"),
            P("pipe", "dp", None),
            P("pipe", "tensor", "dp"),
        ),
        out_specs=P("pipe", "tensor", "dp"),
        check_vma=False,
    )
```

profile of v0, /device:TPU:6, one launch (start us, length us, event | category | flops | bytes accessed | tf_op | source)
XLA Modules:
  0.0 214.8 jit_solution(389587739720034747)
XLA Ops:
  6.5 0.0 copy-start
  6.5 0.0 all-gather.6.cloned.1.call-start
  6.5 0.7 all-gather.6.cloned.1.call-update
  7.3 3.9 %copy.16 = bf16[1,8,1,2,128,512]{4,5,3,2,0,1:T(8,128)(2,1)} copy(bf16[1,8,1,2,128,512]{5,4,3,2,1,0:T(8,128)(2,1)} %param.7) | data formatting | bytes 4194304 | tf_op args[2]
  11.2 0.0 copy-start.1
  11.2 10.4 %all-to-all-start = ((bf16[1,8,1,2,128,512]{4,5,3,2,0,1:T(8,128)(2,1)}), bf16[1,8,1,2,128,512]{4,5,3,2,0,1:T(8,128)(2,1)}, u32[]{:S(2)}, u32[]{:S(2)}) async-start(bf16[1,8,1,2,128,512]{4,5,3,2,0,1:T(8,128)(2,1)} %copy.16), calls=%async_computation.1 | async-start | bytes 4194304 | tf_op jit(solution)/shard_map/all_to_all | solution.py:69
  21.6 0.0 reduce-scatter.3.cloned.1.call-start
  21.7 35.8 %all-gather.6.cloned.1.call-done = bf16[1,1024,1024]{2,1,0:T(8,128)(2,1)} async-done(((bf16[1,128,1024]{2,1,0:T(8,128)(2,1)}), bf16[1,1024,1024]{2,1,0:T(8,128)(2,1)}) %all-gather.6.cloned.1.call-update) | async-done | bytes 2097168 | tf_op jit(solution)/shard_map/all_gather | solution.py:54
  57.5 0.0 copy-done.1
  57.5 4.2 %fusion = f32[1024,512]{1,0:T(8,128)} fusion(bf16[1,1024,1024]{2,1,0:T(8,128)(2,1)} %all-gather.6.cloned.1.call-done, bf16[1,1024,512]{2,1,0:T(8,128)(2,1)S(1)} %copy-done.1), kind=kOutput, calls=%fused_computation | convolution fusion | flops 1073741824 | bytes 5242880 | tf_op jit(solution)/shard_map/dot_general | solution.py:53
  61.7 0.0 reduce-scatter.3.cloned.1.call-update
  61.7 12.1 %all-to-all-done = bf16[1,8,1,2,128,512]{4,5,3,2,0,1:T(8,128)(2,1)} async-done(((bf16[1,8,1,2,128,512]{4,5,3,2,0,1:T(8,128)(2,1)}), bf16[1,8,1,2,128,512]{4,5,3,2,0,1:T(8,128)(2,1)}, u32[]{:S(2)}, u32[]{:S(2)}) %all-to-all-start) | async-done | bytes 2097184 | tf_op jit(solution)/shard_map/all_to_all | solution.py:69
  73.8 0.0 copy-start.2
  73.8 5.0 %all-to-all-start.1 = ((bf16[8,1,1,2,128,512]{4,5,3,2,1,0:T(8,128)(2,1)}), bf16[8,1,1,2,128,512]{4,5,3,2,1,0:T(8,128)(2,1)S(1)}, u32[]{:S(2)}, u32[]{:S(2)}) async-start(bf16[8,1,1,2,128,512]{4,5,3,2,1,0:T(8,128)(2,1)} %bitcast.5), calls=%async_computation.2 | async-start | bytes 4194304 | tf_op jit(solution)/shard_map/all_to_all | solution.py:68
  78.8 0.0 all-gather.4.cloned.1.call-start
  78.8 0.0 copy-done.2
  78.8 0.1 iota_compare_fusion
  78.9 40.9 %all-to-all-done.1 = bf16[8,1,1,2,128,512]{4,5,3,2,1,0:T(8,128)(2,1)S(1)} async-done(((bf16[8,1,1,2,128,512]{4,5,3,2,1,0:T(8,128)(2,1)}), bf16[8,1,1,2,128,512]{4,5,3,2,1,0:T(8,128)(2,1)S(1)}, u32[]{:S(2)}, u32[]{:S(2)}) %all-to-all-start.1) | async-done | bytes 2097184 | tf_op jit(solution)/shard_map/all_to_all | solution.py:68
  119.8 0.1 copy.32
  120.0 0.1 fusion.11
  120.1 0.0 reduce-scatter.3.cloned.1.call-done
  120.1 1.0 convert_element_type.15
  121.1 0.8 broadcast_in_dim.36
  121.9 2.0 reshape_reshape.6
  123.9 1.5 fusion.12
  125.4 0.1 select_reduce_fusion
  125.5 0.7 fusion.4
  126.2 0.1 multiply_reduce_fusion.1
  126.3 1.1 multiply_reduce_fusion
  127.4 0.1 divide_convert_fusion
  127.5 0.1 copy.22
  127.6 0.7 copy.33
  128.3 0.0 all-gather.4.cloned.1.call-update
  128.3 0.0 reduce-scatter.5.cloned.1.call-start
  128.4 33.1 %all-gather.4.cloned.1.call-done = bf16[1024,512]{1,0:T(8,128)(2,1)} async-done(((bf16[128,512]{1,0:T(8,128)(2,1)}), bf16[1024,512]{1,0:T(8,128)(2,1)}) %all-gather.4.cloned.1.call-update) | async-done | bytes 1048592 | tf_op jit(solution)/shard_map/all_gather | solution.py:80
  161.4 0.0 copy-done
  161.5 3.8 %convolution_convert_fusion = bf16[1024,1024]{1,0:T(8,128)(2,1)} fusion(bf16[1024,512]{1,0:T(8,128)(2,1)} %all-gather.4.cloned.1.call-done, bf16[1,512,1024]{2,1,0:T(8,128)(2,1)S(1)} %copy-done), kind=kOutput, calls=%fused_computation.3 | convolution fusion | flops 1074790400 | bytes 4194304 | tf_op jit(solution)/shard_map/dot_general | solution.py:79
  165.3 0.0 reduce-scatter.5.cloned.1.call-update
  165.3 43.0 %reduce-scatter.5.cloned.1.call-done = bf16[128,1024]{1,0:T(8,128)(2,1)} async-done(((bf16[1024,1024]{1,0:T(8,128)(2,1)}), bf16[128,1024]{1,0:T(8,128)(2,1)}) %reduce-scatter.5.cloned.1.call-update) | async-done | bytes 262160 | tf_op jit(solution)/shard_map/reduce_scatter | solution.py:84
Async XLA Ops:
  6.5 154.9 %copy-start = (bf16[1,512,1024]{2,1,0:T(8,128)(2,1)S(1)}, bf16[1,512,1024]{2,1,0:T(8,128)(2,1)}, u32[]{:S(2)}) copy-start(bf16[1,512,1024]{2,1,0:T(8,128)(2,1)} %param.9) | copy-start | bytes 3145732
  6.5 51.0 %all-gather.6.cloned.1.call-start = ((), (), s32[]{:S(2)}) async-start(), calls=%async_computation.7 | async-start | bytes 2359296 | tf_op jit(solution)/shard_map/all_gather | solution.py:54
  11.2 46.3 %copy-start.1 = (bf16[1,1024,512]{2,1,0:T(8,128)(2,1)S(1)}, bf16[1,1024,512]{2,1,0:T(8,128)(2,1)}, u32[]{:S(2)}) copy-start(bf16[1,1024,512]{2,1,0:T(8,128)(2,1)} %param.6) | copy-start | bytes 3145732
  11.2 62.6 %all-to-all-start = ((bf16[1,8,1,2,128,512]{4,5,3,2,0,1:T(8,128)(2,1)}), bf16[1,8,1,2,128,512]{4,5,3,2,0,1:T(8,128)(2,1)}, u32[]{:S(2)}, u32[]{:S(2)}) async-start(bf16[1,8,1,2,128,512]{4,5,3,2,0,1:T(8,128)(2,1)} %copy.16), calls=%async_computation.1 | async-start | bytes 4194304 | tf_op jit(solution)/shard_map/all_to_all | solution.py:69
  21.6 98.5 %reduce-scatter.3.cloned.1.call-start = ((), (), s32[]{:S(2)}) async-start(), calls=%async_computation.4 | async-start | bytes 2359296 | tf_op jit(solution)/shard_map/reduce_scatter | solution.py:58
  73.8 5.0 %copy-start.2 = (s32[1,1,2]{2,1,0:T(1,128)S(1)}, s32[1,1,2]{2,1,0:T(1,128)}, u32[]{:S(2)}) copy-start(s32[1,1,2]{2,1,0:T(1,128)} %param.8) | copy-start | bytes 28
  73.8 46.0 %all-to-all-start.1 = ((bf16[8,1,1,2,128,512]{4,5,3,2,1,0:T(8,128)(2,1)}), bf16[8,1,1,2,128,512]{4,5,3,2,1,0:T(8,128)(2,1)S(1)}, u32[]{:S(2)}, u32[]{:S(2)}) async-start(bf16[8,1,1,2,128,512]{4,5,3,2,1,0:T(8,128)(2,1)} %bitcast.5), calls=%async_computation.2 | async-start | bytes 4194304 | tf_op jit(solution)/shard_map/all_to_all | solution.py:68
  78.8 82.6 %all-gather.4.cloned.1.call-start = ((), (), s32[]{:S(2)}) async-start(), calls=%async_computation.5 | async-start | bytes 1179648 | tf_op jit(solution)/shard_map/all_gather | solution.py:80
  128.3 80.0 %reduce-scatter.5.cloned.1.call-start = ((), (), s32[]{:S(2)}) async-start(), calls=%async_computation.6 | async-start | bytes 2359296 | tf_op jit(solution)/shard_map/reduce_scatter | solution.py:84
Sparse Core Ops, SparseCore 0:
  9.4 48.0 all-gather.5
  61.8 57.2 reduce-scatter.2
  128.4 32.9 all-gather.3
  165.4 42.8 reduce-scatter.4
where the time goes:
time: 215 us
  waiting for transfers between devices  166 us (77%)
  starting transfers between devices  15.5 us (7%)
  between operations  13.2 us (6%)
  matrix products  10.6 us (5%)
  local copies, waits for them, and re-layouts  7.78 us (4%)
    reduce_scatter x1, waiting for transfers between devices, on_device(): lax.psum_scatter(partial_mixed.astype(jnp.bfloat16), 'tensor', scatter_di...  43 us
    all_to_all x1, waiting for transfers between devices, on_device(): lax.all_to_all(lax.all_to_all(neighbour_kv, 'dp', split_axis=1, concat_ax...  40.9 us
    all_gather x1, waiting for transfers between devices, on_device(): lax.all_gather(normed[0], 'tensor', axis=0, tiled=True)  35.8 us
    all_gather x1, waiting for transfers between devices, on_device(): lax.all_gather(attended, 'dp', axis=0, tiled=True)  33.1 us
    all_to_all x1, waiting for transfers between devices, on_device(): lax.all_to_all(neighbour_kv, 'dp', split_axis=1, concat_axis=0, tiled=True)  12.1 us
    all_to_all x1, starting transfers between devices, on_device(): lax.all_to_all(neighbour_kv, 'dp', split_axis=1, concat_axis=0, tiled=True)  10.4 us
    all_to_all x1, starting transfers between devices, on_device(): lax.all_to_all(lax.all_to_all(neighbour_kv, 'dp', split_axis=1, concat_ax...  5.01 us
    unnamed x8, local copies, waits for them, and re-layouts  4.61 us
  transfers between devices with their start and end apart: 6, of which 5 were waited for; matrix products, arithmetic and copies ran while one was open for 4% of the time, Pallas kernels for 0%

commit v1 on v0

v1 whole, which is shorter than its diff:
```python
import math

import jax
import jax.numpy as jnp
from jax import lax
from jax.experimental import pallas as pl
from jax.experimental.pallas import tpu as pltpu
from jax.sharding import PartitionSpec as P

MESH = pl.DeviceIdType.MESH
BF = jnp.bfloat16
F32 = jnp.float32
HD = 128
NEG = -3.0e38
NG = 8
NK = 4
ROWS = 16


def kernel(
    normed, wq_in, kv_in, counts, wo_in, out,
    xg, wq, kv, wo, qp, qin, qfull, po, st, pin, sin, att, ain, pm, rsb, rin, cnt,
    ld_sem, own_send, ag_send, ag_recv, qp_send, qin_recv, xa_send, xa_recv, po_send, st_send, pin_recv, sin_recv,
    at_send, ain_recv, rs_send, rs_recv, cnt_send, cnt_recv,
):
    d = lax.axis_index("dp")
    p = lax.axis_index("pipe")
    t = lax.axis_index("tensor")
    c = p // NK
    k = p % NK
    up = (t + 1) % NG
    dn = (t + NG - 1) % NG
    on_diag = d == p

    def local(src, dst, sem):
        return pltpu.make_async_copy(src, dst, sem)

    def remote(src, dst, ssem, rsem, dev):
        return pltpu.make_async_remote_copy(
            src_ref=src, dst_ref=dst, send_sem=ssem, recv_sem=rsem, device_id=dev, device_id_type=MESH
        )

    def reach(src, dst, ssem, rsem, dev, is_self):
        @pl.when(is_self)
        def _():
            local(src, dst, rsem).start()

        @pl.when(jnp.logical_not(is_self))
        def _():
            remote(src, dst, ssem, rsem, dev).start()

    def await_bytes(ref, sem):
        local(ref, ref, sem).wait()

    loads = [
        local(normed.at[0], xg.at[0, 0], ld_sem.at[0]),
        local(normed.at[1], xg.at[0, 1], ld_sem.at[1]),
        local(wq_in, wq, ld_sem.at[2]),
        local(kv_in, kv, ld_sem.at[3]),
        local(wo_in, wo, ld_sem.at[4]),
    ]
    for load in loads:
        load.start()

    barrier = pltpu.get_barrier_semaphore()

    def greet(dev):
        pl.semaphore_signal(barrier, inc=1, device_id=dev, device_id_type=MESH)

    greet((d, p, up))
    greet((d, p, dn))

    def greet_slots(j, carry):
        greet((d, c * NK + (k + j) % NK, t))
        return carry

    lax.fori_loop(1, NK, greet_slots, 0)

    def greet_plane(j, carry):
        @pl.when(jnp.logical_not(on_diag & (j == p)))
        def _():
            greet((p, j, t))

        @pl.when(jnp.logical_not(on_diag & (j == d)))
        def _():
            greet((j, d, t))

        return carry

    lax.fori_loop(0, NG, greet_plane, 0)

    @pl.when(on_diag)
    def _():
        pl.semaphore_wait(barrier, 2 + 3 + 14)

    @pl.when(jnp.logical_not(on_diag))
    def _():
        pl.semaphore_wait(barrier, 2 + 3 + 16)

    for half in range(2):
        loads[half].wait()
        remote(xg.at[0, half], xg.at[1, half], own_send.at[0, half], ag_recv.at[1, half], (d, p, up)).start()
        remote(xg.at[0, half], xg.at[2, half], own_send.at[1, half], ag_recv.at[2, half], (d, p, dn)).start()

    def send_counts(j, carry):
        b = (j + d) % NG
        reach(counts.at[b // NK], cnt.at[d], cnt_send.at[0], cnt_recv.at[0], (p, b, t), on_diag & (b == p))
        return carry

    lax.fori_loop(0, NG, send_counts, 0)
    loads[2].wait()

    def project(i):
        @pl.when(i >= 1)
        def _():
            upward = i % 2 == 1
            target = (d, p, jnp.where(upward, up, dn))
            later = jnp.minimum(i + 2, NG - 1)
            for half in range(2):
                await_bytes(xg.at[i, half], ag_recv.at[i, half])
                goes = (i <= 5) if half == 0 else ((i <= 4) | (i == 6))

                @pl.when(goes)
                def _():
                    remote(
                        xg.at[i, half], xg.at[later, half], ag_send.at[i, half], ag_recv.at[later, half], target
                    ).start()

        rows = xg[i].reshape(128, 1024)
        part = jnp.dot(rows, wq[...], preferred_element_type=F32).astype(BF)
        qp[i] = part.reshape(NG, ROWS, 512)

        def send(j, carry):
            b = (j + d) % NG
            reach(qp.at[i, b], qin.at[i, d], qp_send.at[i], qin_recv.at[i], (p, b, t), on_diag & (b == p))
            return carry

        lax.fori_loop(0, NG, send, 0)

    def total_query(i):
        await_bytes(qin.at[i], qin_recv.at[i])
        total = qin[i, 0].astype(F32)
        for n in range(1, NG):
            total = total + qin[i, n].astype(F32)
        qfull[i, k] = total.astype(BF)

        def send(j, carry):
            other = c * NK + (k + j) % NK
            remote(qfull.at[i, k], qfull.at[i, k], xa_send.at[i], xa_recv.at[i], (d, other, t)).start()
            return carry

        lax.fori_loop(1, NK, send, 0)

    def sequence_of(i):
        hop = (i + 1) // 2
        return (t + NG + jnp.where(i % 2 == 1, -hop, hop)) % NG

    def attend(i):
        @pl.when(i == 0)
        def _():
            loads[3].wait()
            await_bytes(cnt, cnt_recv.at[0])

        await_bytes(qfull.at[i, pl.ds(0, 3)], xa_recv.at[i])
        g = sequence_of(i)
        lane = lax.broadcasted_iota(jnp.int32, (64, 128), 1)

        def head(h, stats):
            cut = pl.ds(pl.multiple_of(h * HD, HD), HD)
            scores = lax.dot_general(
                qfull[i, :, :, cut].reshape(64, HD), kv[g, 0, :, cut], (((1,), (1,)), ((), ())),
                preferred_element_type=F32,
            ) * (1.0 / math.sqrt(HD))
            top = jnp.max(scores, axis=1, keepdims=True)
            e = jnp.exp(scores - top)
            total = jnp.sum(e, axis=1, keepdims=True)
            o = jnp.dot(e.astype(BF), kv[g, 1, :, cut], preferred_element_type=F32)
            po[i, :, :, cut] = o.astype(BF).reshape(NK, ROWS, HD)
            return jnp.where(lane == h, top, jnp.where(lane == 4 + h, total, stats))

        stats = lax.fori_loop(0, 4, head, jnp.zeros((64, 128), F32))
        stats = jnp.where((lane < 4) & (cnt[g][0:1, :] <= k), NEG, stats)
        st[i] = stats.reshape(NK, ROWS, 128)
        pin[i, k] = po[i, k]
        sin[i, k] = st[i, k]

        def send(j, carry):
            k2 = (k + j) % NK
            dev = (d, c * NK + k2, t)
            remote(po.at[i, k2], pin.at[i, k], po_send.at[i], pin_recv.at[i], dev).start()
            remote(st.at[i, k2], sin.at[i, k], st_send.at[i], sin_recv.at[i], dev).start()
            return carry

        lax.fori_loop(1, NK, send, 0)

    def combine(i):
        await_bytes(pin.at[i, pl.ds(0, 3)], pin_recv.at[i])
        await_bytes(sin.at[i, pl.ds(0, 3)], sin_recv.at[i])
        stats = [sin[i, n] for n in range(NK)]
        top = jnp.maximum(jnp.maximum(stats[0], stats[1]), jnp.maximum(stats[2], stats[3]))
        factor = [jnp.exp(s - top) for s in stats]
        den = factor[0] * pltpu.roll(stats[0], 124, 1)
        for n in range(1, NK):
            den = den + factor[n] * pltpu.roll(stats[n], 124, 1)
        weight = [f / den for f in factor]
        for h in range(4):
            cut = slice(h * HD, (h + 1) * HD)
            num = weight[0][:, h:h + 1] * pin[i, 0, :, cut].astype(F32)
            for n in range(1, NK):
                num = num + weight[n][:, h:h + 1] * pin[i, n, :, cut].astype(F32)
            att[i, :, cut] = num.astype(BF)

        def send(j, carry):
            d2 = (j + p) % NG
            reach(att.at[i], ain.at[i, p], at_send.at[i], ain_recv.at[i], (d2, d, t), on_diag & (d2 == d))
            return carry

        lax.fori_loop(0, NG, send, 0)

    def mix(i):
        @pl.when(i == 0)
        def _():
            loads[4].wait()

        await_bytes(ain.at[i], ain_recv.at[i])
        pm[i] = jnp.dot(ain[i].reshape(128, 512), wo[...], preferred_element_type=F32)

    def step(i, carry):
        for lag, stage in enumerate((project, total_query, attend, combine, mix)):
            @pl.when((i >= lag) & (i - lag < NG))
            def _():
                stage(i - lag)

        return carry

    lax.fori_loop(0, NG + 4, step, 0)

    def pass_on(slot, half, later, tensor_to, incoming):
        mine = pm[slot, :, half * 512:(half + 1) * 512]
        if incoming:
            await_bytes(rin.at[slot, half], rs_recv.at[slot, half])
            mine = mine + rin[slot, half].astype(F32)
        rsb[slot, half] = mine.astype(BF)
        remote(
            rsb.at[slot, half], rin.at[later, half], rs_send.at[slot, half], rs_recv.at[later, half],
            (d, p, tensor_to),
        ).start()

    pass_on(7, 0, 5, dn, False)
    pass_on(7, 1, 6, up, False)
    pass_on(5, 1, 3, dn, False)
    pass_on(6, 0, 4, up, False)
    pass_on(5, 0, 3, dn, True)
    pass_on(6, 1, 4, up, True)
    for half in range(2):
        pass_on(3, 1 - half, 1, dn, True)
        pass_on(4, half, 2, up, True)
    for half in range(2):
        pass_on(1, 1 - half, 0, dn, True)
        pass_on(2, half, 7, up, True)
    for half in range(2):
        await_bytes(rin.at[0, half], rs_recv.at[0, half])
        await_bytes(rin.at[7, half], rs_recv.at[7, half])
        cut = slice(half * 512, (half + 1) * 512)
        out[:, cut] = (pm[0, :, cut] + rin[0, half].astype(F32) + rin[7, half].astype(F32)).astype(BF)

    for way in range(2):
        for half in range(2):
            await_bytes(xg.at[0, half], own_send.at[way, half])
    for i in range(1, 7):
        for half in range(2):
            if (half == 0 and i <= 5) or (half == 1 and i != 5):
                await_bytes(xg.at[i, half], ag_send.at[i, half])
    for slot in range(1, NG):
        for half in range(2):
            await_bytes(rsb.at[slot, half], rs_send.at[slot, half])

    @pl.when(on_diag)
    def _():
        await_bytes(cnt.at[pl.ds(0, 7)], cnt_send.at[0])

    @pl.when(jnp.logical_not(on_diag))
    def _():
        await_bytes(cnt, cnt_send.at[0])

    def drain(i, carry):
        await_bytes(qfull.at[i, pl.ds(0, 3)], xa_send.at[i])
        await_bytes(po.at[i, pl.ds(0, 3)], po_send.at[i])
        await_bytes(st.at[i, pl.ds(0, 3)], st_send.at[i])

        @pl.when(on_diag)
        def _():
            await_bytes(qp.at[i, pl.ds(0, 7)], qp_send.at[i])
            await_bytes(ain.at[i, pl.ds(0, 7)], at_send.at[i])

        @pl.when(jnp.logical_not(on_diag))
        def _():
            await_bytes(qp.at[i], qp_send.at[i])
            await_bytes(ain.at[i], at_send.at[i])

        return carry

    lax.fori_loop(0, NG, drain, 0)


def on_device(normed, w_query, neighbour_kv, counts, w_out):
    dma = pltpu.SemaphoreType.DMA
    anywhere = pl.BlockSpec(memory_space=pl.ANY)
    return pl.pallas_call(
        kernel,
        out_shape=jax.ShapeDtypeStruct((128, 1024), BF),
        in_specs=[anywhere, anywhere, anywhere, pl.BlockSpec(memory_space=pltpu.VMEM), anywhere],
        out_specs=pl.BlockSpec(memory_space=pltpu.VMEM),
        scratch_shapes=[
            pltpu.VMEM((NG, 2, 64, 1024), BF),
            pltpu.VMEM((1024, 512), BF),
            pltpu.VMEM((NG, 2, 128, 512), BF),
            pltpu.VMEM((512, 1024), BF),
            pltpu.VMEM((NG, NG, ROWS, 512), BF),
            pltpu.VMEM((NG, NG, ROWS, 512), BF),
            pltpu.VMEM((NG, NK, ROWS, 512), BF),
            pltpu.VMEM((NG, NK, ROWS, 512), BF),
            pltpu.VMEM((NG, NK, ROWS, 128), F32),
            pltpu.VMEM((NG, NK, ROWS, 512), BF),
            pltpu.VMEM((NG, NK, ROWS, 128), F32),
            pltpu.VMEM((NG, ROWS, 512), BF),
            pltpu.VMEM((NG, NG, ROWS, 512), BF),
            pltpu.VMEM((NG, 128, 1024), F32),
            pltpu.VMEM((NG, 2, 128, 512), BF),
            pltpu.VMEM((NG, 2, 128, 512), BF),
            pltpu.VMEM((NG, 8, 128), jnp.int32),
            dma((5,)), dma((2, 2)), dma((NG, 2)), dma((NG, 2)),
            dma((NG,)), dma((NG,)), dma((NG,)), dma((NG,)),
            dma((NG,)), dma((NG,)), dma((NG,)), dma((NG,)),
            dma((NG,)), dma((NG,)), dma((NG, 2)), dma((NG, 2)),
            dma((1,)), dma((1,)),
        ],
        compiler_params=pltpu.CompilerParams(
            collective_id=0, has_side_effects=True, vmem_limit_bytes=60 * 1024 * 1024
        ),
        cost_estimate=pl.CostEstimate(flops=2_500_000_000, bytes_accessed=5_000_000, transcendentals=300_000),
    )(
        normed.reshape(2, 64, 1024),
        w_query.reshape(1024, 512),
        neighbour_kv.reshape(NG, 2, 128, 512),
        jnp.broadcast_to(counts.reshape(2, 1, 1), (2, 8, 128)),
        w_out.reshape(512, 1024),
    )[None]


def solution(mesh):
    return jax.shard_map(
        on_device,
        mesh=mesh,
        in_specs=(
            P("pipe", "tensor", "dp"),
            P("pipe", "dp", "tensor"),
            P("dp", None, "pipe", None, None, "tensor"),
            P("pipe", "dp", None),
            P("pipe", "tensor", "dp"),
        ),
        out_specs=P("pipe", "tensor", "dp"),
        check_vma=False,
    )
```

time: 215 us -> 122 us (0.57)
  the two profiles are of different devices: /device:TPU:6 before, /device:TPU:64 now
where the time goes in v1:
time: 122 us; the launch traced here: 121 us
  Pallas kernels  118 us (97%)
  local copies, waits for them, and re-layouts  2.99 us (2%)
    pallas_call x1, Pallas kernels, on_device(): pl.pallas_call(kernel, out_shape=jax.ShapeDtypeStruct((128, 1024), BF), i...  118 us

profile of v1, /device:TPU:64, one launch (start us, length us, event | category | flops | bytes accessed | tf_op | source)
XLA Modules:
  0.0 121.4 jit_solution(1450062970483373520)
XLA Ops:
  0.0 1.3 %broadcast_in_dim.11.counts = s32[2,8,128]{2,1,0:T(8,128)} broadcast(s32[2]{0:T(128)} %bitcast.7), dimensions={0} | broadcast | bytes 8200 | tf_op jit(solution)/shard_map/broadcast_in_dim | solution.py:346
  1.3 118.3 %shard_map.55 = bf16[128,1024]{1,0:T(8,128)(2,1)} custom-call(bf16[2,64,1024]{2,1,0:T(8,128)(2,1)} %bitcast.11, bf16[1024,512]{1,0:T(8,128)(2,1)} %bitcast.9, bf16[8,2,128,512]{3,2,1,0:T(8,128)(2,1)} %bitcast.8, s32[2,8,128]{2,1,0:T(8,128)} %broadcast_in_dim.11.counts, bf16[512,1024]{1,0:T(8,128)(2,1)} %bitcast.10), custom_call_target="tpu_custom_call" | custom-call | flops 2500000000 | bytes 5000000 | tf_op jit(solution)/shard_map/pallas_call | solution.py:309
  119.7 1.7 %copy.7 = bf16[1,128,1024]{2,1,0:T(8,128)(2,1)} copy(bf16[1,128,1024]{2,1,0:T(8,128)(2,1)} %bitcast.6) | data formatting | bytes 524288

commit v2 on v1

v2 whole, which is shorter than its diff:
```python
import math

import jax
import jax.numpy as jnp
from jax import lax
from jax.experimental import pallas as pl
from jax.experimental.pallas import tpu as pltpu
from jax.sharding import PartitionSpec as P

MESH = pl.DeviceIdType.MESH
BF = jnp.bfloat16
F32 = jnp.float32
HD = 128
NEG = -3.0e38
NG = 8
NK = 4
ROWS = 16
UNITS = 2 * NG
LAGS = (0, 2, 4, 6, 8, 10, 12, 14)
BY_SPAN = False
RING_AT = {}


def kernel(
    normed, wq_in, kv_in, counts, wo_in, out,
    xg, wq, kv, wo, qp, sib, qs, qin, qfull, po, st, pin, sin, att, ain, pm, rsb, rin, cnt_two, cnt,
    ld_sem, own_send, ag_send, ag_recv, sib_send, sib_recv, qs_send, qin_recv, xa_send, xa_recv,
    po_send, st_send, pin_recv, sin_recv, at_send, at_recv, sp_send, sp_recv, fw_send, fw_recv,
    rs_send, rs_recv, c2_send, c2_recv, cnt_send, cnt_recv,
):
    d = lax.axis_index("dp")
    p = lax.axis_index("pipe")
    t = lax.axis_index("tensor")
    zh = d // 2
    co = d % 2
    sibling = d + 1 - 2 * co
    c_own = p // NK
    k = p % NK
    up = (t + 1) % NG
    dn = (t + NG - 1) % NG
    on_diag = d == p
    query_self = on_diag & (k // 2 == co)
    spread_self = on_diag & (2 * k + c_own == d)

    def local(src, dst, sem):
        return pltpu.make_async_copy(src, dst, sem)

    def remote(src, dst, ssem, rsem, dev):
        return pltpu.make_async_remote_copy(
            src_ref=src, dst_ref=dst, send_sem=ssem, recv_sem=rsem, device_id=dev, device_id_type=MESH
        )

    def reach(src, dst, ssem, rsem, dev, is_self):
        @pl.when(is_self)
        def _():
            local(src, dst, rsem).start()

        @pl.when(jnp.logical_not(is_self))
        def _():
            remote(src, dst, ssem, rsem, dev).start()

    def await_bytes(ref, sem):
        local(ref, ref, sem).wait()

    loads = [
        local(normed.at[0], xg.at[0, 0], ld_sem.at[0]),
        local(normed.at[1], xg.at[0, 1], ld_sem.at[1]),
        local(wq_in, wq, ld_sem.at[2]),
        local(kv_in, kv, ld_sem.at[3]),
        local(wo_in, wo, ld_sem.at[4]),
    ]
    for load in loads:
        load.start()

    barrier = pltpu.get_barrier_semaphore()

    def greet(dev):
        pl.semaphore_signal(barrier, inc=1, device_id=dev, device_id_type=MESH)

    def greet_other(dev, is_self):
        @pl.when(jnp.logical_not(is_self))
        def _():
            greet(dev)

    greet((d, p, up))
    greet((d, p, dn))
    for n in range(NK):
        b = (n % 2) * NK + 2 * co + n // 2
        greet_other((p, b, t), on_diag & (b == p))
        source = 2 * n + k // 2
        greet_other((source, d, t), on_diag & (source == d))
    greet_other((2 * k + c_own, d, t), spread_self)
    greet_other((p, NK * co + zh, t), spread_self)
    for n in range(1, NK):
        greet((d, c_own * NK + (k + n) % NK, t))
        greet((((zh + n) % NK) * 2 + co, p, t))
    greet((sibling, p, t))
    for span in range(2):
        cnt_two[span, co] = jnp.full((8, 128), counts[0, 0, span], jnp.int32)
    pl.semaphore_wait(barrier, 19 - 2 * jnp.where(query_self, 1, 0) - 2 * jnp.where(spread_self, 1, 0))

    for half in range(2):
        loads[half].wait()
        remote(xg.at[0, half], xg.at[1, half], own_send.at[0, half], ag_recv.at[1, half], (d, p, up)).start()
        remote(xg.at[0, half], xg.at[2, half], own_send.at[1, half], ag_recv.at[2, half], (d, p, dn)).start()
    for span in range(2):
        remote(
            cnt_two.at[span, co], cnt_two.at[span, co], c2_send.at[span], c2_recv.at[span], (sibling, p, t)
        ).start()
    loads[2].wait()

    def project(c, i):
        @pl.when(i >= 1)
        def _():
            await_bytes(xg.at[i, c], ag_recv.at[i, c])
            upward = i % 2 == 1
            target = (d, p, jnp.where(upward, up, dn))
            later = jnp.minimum(i + 2, NG - 1)

            @pl.when((i <= 4) | (i == 5 + c))
            def _():
                remote(xg.at[i, c], xg.at[later, c], ag_send.at[i, c], ag_recv.at[later, c], target).start()

        part = jnp.dot(xg[i, c], wq[...], preferred_element_type=F32).astype(BF)
        qp[c, i] = part.reshape(NK, ROWS, 512)
        remote(
            qp.at[c, i, pl.ds(2 - 2 * co, 2)], sib.at[c, i], sib_send.at[c, i], sib_recv.at[c, i], (sibling, p, t)
        ).start()

    def join_cores(c, i):
        @pl.when(i == 0)
        def _():
            await_bytes(cnt_two.at[c, co], c2_recv.at[c])
            for n in range(2):
                b = c * NK + 2 * co + n
                reach(cnt_two.at[c], cnt.at[zh], cnt_send.at[c], cnt_recv.at[0], (p, b, t), on_diag & (b == p))

        await_bytes(sib.at[c, i], sib_recv.at[c, i])
        for n in range(2):
            b = c * NK + 2 * co + n
            qs[c, i, n] = (qp[c, i, 2 * co + n].astype(F32) + sib[c, i, n].astype(F32)).astype(BF)
            reach(qs.at[c, i, n], qin.at[i, zh], qs_send.at[c, i], qin_recv.at[i], (p, b, t), on_diag & (b == p))

    def total_query(c, i):
        await_bytes(qin.at[i], qin_recv.at[i])
        total = qin[i, 0].astype(F32)
        for n in range(1, NK):
            total = total + qin[i, n].astype(F32)
        qfull[i, k] = total.astype(BF)
        for n in range(1, NK):
            dev = (d, c_own * NK + (k + n) % NK, t)
            remote(qfull.at[i, k], qfull.at[i, k], xa_send.at[i], xa_recv.at[i], dev).start()

    def sequence_of(i):
        hop = (i + 1) // 2
        return (t + NG + jnp.where(i % 2 == 1, -hop, hop)) % NG

    def attend(c, i):
        @pl.when(i == 0)
        def _():
            loads[3].wait()
            await_bytes(cnt, cnt_recv.at[0])

        await_bytes(qfull.at[i, pl.ds(0, 3)], xa_recv.at[i])
        g = sequence_of(i)
        lane = lax.broadcasted_iota(jnp.int32, (64, 128), 1)
        stats = jnp.zeros((64, 128), F32)
        for h in range(4):
            cut = slice(h * HD, (h + 1) * HD)
            scores = lax.dot_general(
                qfull[i, :, :, cut].reshape(64, HD), kv[g, 0, :, cut], (((1,), (1,)), ((), ())),
                preferred_element_type=F32,
            ) * (1.0 / math.sqrt(HD))
            top = jnp.max(scores, axis=1, keepdims=True)
            e = jnp.exp(scores - top)
            total = jnp.sum(e, axis=1, keepdims=True)
            o = jnp.dot(e.astype(BF), kv[g, 1, :, cut], preferred_element_type=F32)
            po[i, :, :, cut] = o.astype(BF).reshape(NK, ROWS, HD)
            stats = jnp.where(lane == h, top, stats)
            stats = jnp.where(lane == 4 + h, total, stats)
        stats = jnp.where((lane < 4) & (cnt[g // 2, g % 2][0:1, :] <= k), NEG, stats)
        st[i] = stats.reshape(NK, ROWS, 128)
        pin[i, k] = po[i, k]
        sin[i, k] = st[i, k]
        for n in range(1, NK):
            k2 = (k + n) % NK
            dev = (d, c_own * NK + k2, t)
            remote(po.at[i, k2], pin.at[i, k], po_send.at[i], pin_recv.at[i], dev).start()
            remote(st.at[i, k2], sin.at[i, k], st_send.at[i], sin_recv.at[i], dev).start()

    def combine(c, i):
        await_bytes(pin.at[i, pl.ds(0, 3)], pin_recv.at[i])
        await_bytes(sin.at[i, pl.ds(0, 3)], sin_recv.at[i])
        stats = [sin[i, n] for n in range(NK)]
        top = jnp.maximum(jnp.maximum(stats[0], stats[1]), jnp.maximum(stats[2], stats[3]))
        factor = [jnp.exp(s - top) for s in stats]
        den = factor[0] * pltpu.roll(stats[0], 124, 1)
        for n in range(1, NK):
            den = den + factor[n] * pltpu.roll(stats[n], 124, 1)
        weight = [f / den for f in factor]
        for h in range(4):
            cut = slice(h * HD, (h + 1) * HD)
            num = weight[0][:, h:h + 1] * pin[i, 0, :, cut].astype(F32)
            for n in range(1, NK):
                num = num + weight[n][:, h:h + 1] * pin[i, n, :, cut].astype(F32)
            att[i, :, cut] = num.astype(BF)
        reach(att.at[i], ain.at[c_own, i, k], at_send.at[i], at_recv.at[i], (2 * k + c_own, d, t), spread_self)

    def spread(c, i):
        await_bytes(att.at[i], at_recv.at[i])
        for n in range(1, NK):
            dev = (((zh + n) % NK) * 2 + co, p, t)
            remote(ain.at[co, i, zh], ain.at[co, i, zh], sp_send.at[i], sp_recv.at[i], dev).start()

    def hand_over(c, i):
        await_bytes(ain.at[co, i, pl.ds(0, 3)], sp_recv.at[i])
        remote(ain.at[co, i], ain.at[co, i], fw_send.at[i], fw_recv.at[i], (sibling, p, t)).start()

    def mix(c, i):
        @pl.when((c == 0) & (i == 0))
        def _():
            loads[4].wait()

        @pl.when(co != c)
        def _():
            await_bytes(ain.at[c, i], fw_recv.at[i])

        pm[c, i] = jnp.dot(ain[c, i].reshape(64, 512), wo[...], preferred_element_type=F32)

    def pass_on(c, slot, later, tensor_to, incoming):
        mine = pm[c, slot]
        if incoming:
            await_bytes(rin.at[c, slot], rs_recv.at[c, slot])
            mine = mine + rin[c, slot].astype(F32)
        rsb[c, slot] = mine.astype(BF)
        remote(
            rsb.at[c, slot], rin.at[c, later], rs_send.at[c, slot], rs_recv.at[c, later], (d, p, tensor_to)
        ).start()

    def ring(c, r):
        down = {1: (5, 3), 2: (3, 1), 3: (1, 0)}
        upward = {1: (6, 4), 2: (4, 2), 3: (2, 7)}
        if r == 0 and c == 0:
            pass_on(c, 7, 5, dn, False)
            pass_on(c, 6, 4, up, False)
        elif r == 0:
            pass_on(c, 7, 6, up, False)
            pass_on(c, 5, 3, dn, False)
        elif r == 1 and c == 0:
            pass_on(c, *down[r], dn, True)
        elif r == 1:
            pass_on(c, *upward[r], up, True)
        elif r < 4:
            pass_on(c, *down[r], dn, True)
            pass_on(c, *upward[r], up, True)
        else:
            await_bytes(rin.at[c, 0], rs_recv.at[c, 0])
            await_bytes(rin.at[c, 7], rs_recv.at[c, 7])
            out[c * 64:(c + 1) * 64] = (pm[c, 0] + rin[c, 0].astype(F32) + rin[c, 7].astype(F32)).astype(BF)

    stages = (
        (project, None), (join_cores, None), (total_query, c_own), (attend, c_own), (combine, c_own),
        (spread, co), (hand_over, co), (mix, None),
    )

    def step(u, carry):
        for lag, (stage, only) in zip(LAGS, stages):
            v = u - lag
            c, i = (v // NG, v % NG) if BY_SPAN else (v % 2, v // 2)
            run = (v >= 0) & (v < UNITS)

            @pl.when(run if only is None else run & (c == only))
            def _():
                stage(c, i)

        for (c, r), at in RING_AT.items():
            @pl.when(u == at)
            def _():
                ring(c, r)

        return carry

    lax.fori_loop(0, UNITS + LAGS[-1], step, 0)
    for r in range(5):
        for c in range(2):
            if (c, r) not in RING_AT:
                ring(c, r)

    for way in range(2):
        for half in range(2):
            await_bytes(xg.at[0, half], own_send.at[way, half])
    for i in range(1, 7):
        for half in range(2):
            if i <= 4 or i == 5 + half:
                await_bytes(xg.at[i, half], ag_send.at[i, half])
    for c in range(2):
        await_bytes(cnt_two.at[c, co], c2_send.at[c])

    def drain(i, carry):
        for c in range(2):
            @pl.when(i >= 1)
            def _():
                await_bytes(rsb.at[c, i], rs_send.at[c, i])

            await_bytes(sib.at[c, i], sib_send.at[c, i])
            one_less = query_self & (c == c_own)

            @pl.when(one_less)
            def _():
                await_bytes(qs.at[c, i, 0], qs_send.at[c, i])

            @pl.when(jnp.logical_not(one_less))
            def _():
                await_bytes(qs.at[c, i], qs_send.at[c, i])

            @pl.when((i == 0) & one_less)
            def _():
                await_bytes(cnt.at[0], cnt_send.at[c])

            @pl.when((i == 0) & jnp.logical_not(one_less))
            def _():
                await_bytes(cnt.at[pl.ds(0, 2)], cnt_send.at[c])

        await_bytes(qfull.at[i, pl.ds(0, 3)], xa_send.at[i])
        await_bytes(po.at[i, pl.ds(0, 3)], po_send.at[i])
        await_bytes(st.at[i, pl.ds(0, 3)], st_send.at[i])

        @pl.when(jnp.logical_not(spread_self))
        def _():
            await_bytes(att.at[i], at_send.at[i])

        await_bytes(ain.at[0, i, pl.ds(0, 3)], sp_send.at[i])
        await_bytes(ain.at[0, i], fw_send.at[i])
        return carry

    lax.fori_loop(0, NG, drain, 0)


def on_device(normed, w_query, neighbour_kv, counts, w_out):
    dma = pltpu.SemaphoreType.DMA
    anywhere = pl.BlockSpec(memory_space=pl.ANY)
    both = dma((2, NG))
    one = dma((NG,))
    return pl.pallas_call(
        kernel,
        out_shape=jax.ShapeDtypeStruct((128, 1024), BF),
        in_specs=[anywhere, anywhere, anywhere, pl.BlockSpec(memory_space=pltpu.SMEM), anywhere],
        out_specs=pl.BlockSpec(memory_space=pltpu.VMEM),
        scratch_shapes=[
            pltpu.VMEM((NG, 2, 64, 1024), BF),
            pltpu.VMEM((1024, 512), BF),
            pltpu.VMEM((NG, 2, 128, 512), BF),
            pltpu.VMEM((512, 1024), BF),
            pltpu.VMEM((2, NG, NK, ROWS, 512), BF),
            pltpu.VMEM((2, NG, 2, ROWS, 512), BF),
            pltpu.VMEM((2, NG, 2, ROWS, 512), BF),
            pltpu.VMEM((NG, NK, ROWS, 512), BF),
            pltpu.VMEM((NG, NK, ROWS, 512), BF),
            pltpu.VMEM((NG, NK, ROWS, 512), BF),
            pltpu.VMEM((NG, NK, ROWS, 128), F32),
            pltpu.VMEM((NG, NK, ROWS, 512), BF),
            pltpu.VMEM((NG, NK, ROWS, 128), F32),
            pltpu.VMEM((NG, ROWS, 512), BF),
            pltpu.VMEM((2, NG, NK, ROWS, 512), BF),
            pltpu.VMEM((2, NG, 64, 1024), F32),
            pltpu.VMEM((2, NG, 64, 1024), BF),
            pltpu.VMEM((2, NG, 64, 1024), BF),
            pltpu.VMEM((2, 2, 8, 128), jnp.int32),
            pltpu.VMEM((NK, 2, 8, 128), jnp.int32),
            dma((5,)), dma((2, 2)), dma((NG, 2)), dma((NG, 2)),
            both, both, both, one, one, one,
            one, one, one, one, one, one, one, one, one, one,
            both, both, dma((2,)), dma((2,)), dma((2,)), dma((1,)),
        ],
        compiler_params=pltpu.CompilerParams(
            collective_id=0, has_side_effects=True, vmem_limit_bytes=60 * 1024 * 1024
        ),
        cost_estimate=pl.CostEstimate(flops=2_500_000_000, bytes_accessed=5_000_000, transcendentals=300_000),
    )(
        normed.reshape(2, 64, 1024),
        w_query.reshape(1024, 512),
        neighbour_kv.reshape(NG, 2, 128, 512),
        counts,
        w_out.reshape(512, 1024),
    )[None]


def solution(mesh):
    return jax.shard_map(
        on_device,
        mesh=mesh,
        in_specs=(
            P("pipe", "tensor", "dp"),
            P("pipe", "dp", "tensor"),
            P("dp", None, "pipe", None, None, "tensor"),
            P("pipe", "dp", None),
            P("pipe", "tensor", "dp"),
        ),
        out_specs=P("pipe", "tensor", "dp"),
        check_vma=False,
    )
```

time: 122 us -> 113 us (0.926)
  the two profiles are of different devices: /device:TPU:64 before, /device:TPU:1 now
where the time goes in v2:
time: 113 us; the launch traced here: 112 us
  Pallas kernels  111 us (98%)
  local copies, waits for them, and re-layouts  1.67 us (1%)
    pallas_call x1, Pallas kernels, on_device(): pl.pallas_call(kernel, out_shape=jax.ShapeDtypeStruct((128, 1024), BF), i...  111 us

profile of v2, /device:TPU:1, one launch (start us, length us, event | category | flops | bytes accessed | tf_op | source)
XLA Modules:
  0.0 112.5 jit_solution(11472494254813823478)
XLA Ops:
  0.0 110.8 %shard_map.55 = bf16[128,1024]{1,0:T(8,128)(2,1)} custom-call(bf16[2,64,1024]{2,1,0:T(8,128)(2,1)} %bitcast.9, bf16[1024,512]{1,0:T(8,128)(2,1)} %bitcast.7, bf16[8,2,128,512]{3,2,1,0:T(8,128)(2,1)} %bitcast.6, s32[1,1,2]{2,1,0:T(1,128)} %counts.1, bf16[512,1024]{1,0:T(8,128)(2,1)} %bitcast.8), custom_call_target="tpu_custom_call" | custom-call | flops 2500000000 | bytes 5000000 | tf_op jit(solution)/shard_map/pallas_call | solution.py:344
  110.8 1.7 %copy.7 = bf16[1,128,1024]{2,1,0:T(8,128)(2,1)} copy(bf16[1,128,1024]{2,1,0:T(8,128)(2,1)} %bitcast.5) | data formatting | bytes 524288

commit v3 on v2

--- a/solution.py
+++ b/solution.py
@@ -14,19 +14,17 @@
 NEG = -3.0e38
 NG = 8
 NK = 4
-ROWS = 16
 UNITS = 2 * NG
-LAGS = (0, 2, 4, 6, 8, 10, 12, 14)
+LAGS = (0, 2, 5, 8, 10)
 BY_SPAN = False
 RING_AT = {}
 
 
 def kernel(
     normed, wq_in, kv_in, counts, wo_in, out,
-    xg, wq, kv, wo, qp, sib, qs, qin, qfull, po, st, pin, sin, att, ain, pm, rsb, rin, cnt_two, cnt,
-    ld_sem, own_send, ag_send, ag_recv, sib_send, sib_recv, qs_send, qin_recv, xa_send, xa_recv,
-    po_send, st_send, pin_recv, sin_recv, at_send, at_recv, sp_send, sp_recv, fw_send, fw_recv,
-    rs_send, rs_recv, c2_send, c2_recv, cnt_send, cnt_recv,
+    xg, wq, kv, kvh, wo, qp, sib, qs, qin, att, ain, pm, rsb, rin, cnt_two, cnt,
+    ld_sem, own_send, ag_send, ag_recv, sib_send, sib_recv, qs_send, qin_recv, kv_own, kv_send, kv_recv,
+    at_send, at_recv, fw_send, fw_recv, rs_send, rs_recv, c2_send, c2_recv, cnt_send, cnt_recv,
 ):
     d = lax.axis_index("dp")
     p = lax.axis_index("pipe")
@@ -40,7 +38,6 @@
     dn = (t + NG - 1) % NG
     on_diag = d == p
     query_self = on_diag & (k // 2 == co)
-    spread_self = on_diag & (2 * k + c_own == d)
 
     def local(src, dst, sem):
         return pltpu.make_async_copy(src, dst, sem)
@@ -89,15 +86,12 @@
         greet_other((p, b, t), on_diag & (b == p))
         source = 2 * n + k // 2
         greet_other((source, d, t), on_diag & (source == d))
-    greet_other((2 * k + c_own, d, t), spread_self)
-    greet_other((p, NK * co + zh, t), spread_self)
     for n in range(1, NK):
         greet((d, c_own * NK + (k + n) % NK, t))
-        greet((((zh + n) % NK) * 2 + co, p, t))
     greet((sibling, p, t))
     for span in range(2):
         cnt_two[span, co] = jnp.full((8, 128), counts[0, 0, span], jnp.int32)
-    pl.semaphore_wait(barrier, 19 - 2 * jnp.where(query_self, 1, 0) - 2 * jnp.where(spread_self, 1, 0))
+    pl.semaphore_wait(barrier, 14 - 2 * jnp.where(query_self, 1, 0))
 
     for half in range(2):
         loads[half].wait()
@@ -107,6 +101,27 @@
         remote(
             cnt_two.at[span, co], cnt_two.at[span, co], c2_send.at[span], c2_recv.at[span], (sibling, p, t)
         ).start()
+    loads[3].wait()
+
+    def sequence_of(i):
+        hop = (i + 1) // 2
+        return (t + NG + jnp.where(i % 2 == 1, -hop, hop)) % NG
+
+    def head_of(n):
+        return pl.ds(pl.multiple_of(n * HD, HD), HD)
+
+    def send_heads(i, carry):
+        g = sequence_of(i)
+        local(kv.at[g, :, :, head_of(k)], kvh.at[i, :, k], kv_own.at[i]).start()
+        for n in range(1, NK):
+            k2 = (k + n) % NK
+            remote(
+                kv.at[g, :, :, head_of(k2)], kvh.at[i, :, k], kv_send.at[i], kv_recv.at[i],
+                (d, c_own * NK + k2, t),
+            ).start()
+        return carry
+
+    lax.fori_loop(0, NG, send_heads, 0)
     loads[2].wait()
 
     def project(c, i):
@@ -122,7 +137,8 @@
                 remote(xg.at[i, c], xg.at[later, c], ag_send.at[i, c], ag_recv.at[later, c], target).start()
 
         part = jnp.dot(xg[i, c], wq[...], preferred_element_type=F32).astype(BF)
-        qp[c, i] = part.reshape(NK, ROWS, 512)
+        for h in range(NK):
+            qp[c, i, h] = part[:, h * HD:(h + 1) * HD]
         remote(
             qp.at[c, i, pl.ds(2 - 2 * co, 2)], sib.at[c, i], sib_send.at[c, i], sib_recv.at[c, i], (sibling, p, t)
         ).start()
@@ -141,91 +157,55 @@
             qs[c, i, n] = (qp[c, i, 2 * co + n].astype(F32) + sib[c, i, n].astype(F32)).astype(BF)
             reach(qs.at[c, i, n], qin.at[i, zh], qs_send.at[c, i], qin_recv.at[i], (p, b, t), on_diag & (b == p))
 
-    def total_query(c, i):
+    def attend(c, i):
+        @pl.when(i == 0)
+        def _():
+            await_bytes(cnt, cnt_recv.at[0])
+
+        await_bytes(kvh.at[i, :, 0], kv_own.at[i])
+        await_bytes(kvh.at[i, :, pl.ds(0, 3)], kv_recv.at[i])
         await_bytes(qin.at[i], qin_recv.at[i])
         total = qin[i, 0].astype(F32)
         for n in range(1, NK):
             total = total + qin[i, n].astype(F32)
-        qfull[i, k] = total.astype(BF)
+        q = total.astype(BF)
+        g = sequence_of(i)
+        count = cnt[g // 2, g % 2][0:1, :]
+        scores = []
+        for n in range(NK):
+            s = lax.dot_general(
+                q, kvh[i, 0, n], (((1,), (1,)), ((), ())), preferred_element_type=F32
+            ) * (1.0 / math.sqrt(HD))
+            scores.append(jnp.where(count > n, s, NEG))
+        top = jnp.max(
+            jnp.maximum(jnp.maximum(scores[0], scores[1]), jnp.maximum(scores[2], scores[3])), axis=1, keepdims=True
+        )
+        e = [jnp.exp(s - top) for s in scores]
+        den = jnp.sum((e[0] + e[1]) + (e[2] + e[3]), axis=1, keepdims=True)
+        o = jnp.dot(e[0].astype(BF), kvh[i, 1, 0], preferred_element_type=F32)
         for n in range(1, NK):
-            dev = (d, c_own * NK + (k + n) % NK, t)
-            remote(qfull.at[i, k], qfull.at[i, k], xa_send.at[i], xa_recv.at[i], dev).start()
-
-    def sequence_of(i):
-        hop = (i + 1) // 2
-        return (t + NG + jnp.where(i % 2 == 1, -hop, hop)) % NG
-
-    def attend(c, i):
-        @pl.when(i == 0)
-        def _():
-            loads[3].wait()
-            await_bytes(cnt, cnt_recv.at[0])
-
-        await_bytes(qfull.at[i, pl.ds(0, 3)], xa_recv.at[i])
-        g = sequence_of(i)
-        lane = lax.broadcasted_iota(jnp.int32, (64, 128), 1)
-        stats = jnp.zeros((64, 128), F32)
-        for h in range(4):
-            cut = slice(h * HD, (h + 1) * HD)
-            scores = lax.dot_general(
-                qfull[i, :, :, cut].reshape(64, HD), kv[g, 0, :, cut], (((1,), (1,)), ((), ())),
-                preferred_element_type=F32,
-            ) * (1.0 / math.sqrt(HD))
-            top = jnp.max(scores, axis=1, keepdims=True)
-            e = jnp.exp(scores - top)
-            total = jnp.sum(e, axis=1, keepdims=True)
-            o = jnp.dot(e.astype(BF), kv[g, 1, :, cut], preferred_element_type=F32)
-            po[i, :, :, cut] = o.astype(BF).reshape(NK, ROWS, HD)
-            stats = jnp.where(lane == h, top, stats)
-            stats = jnp.where(lane == 4 + h, total, stats)
-        stats = jnp.where((lane < 4) & (cnt[g // 2, g % 2][0:1, :] <= k), NEG, stats)
-        st[i] = stats.reshape(NK, ROWS, 128)
-        pin[i, k] = po[i, k]
-        sin[i, k] = st[i, k]
-        for n in range(1, NK):
-            k2 = (k + n) % NK
-            dev = (d, c_own * NK + k2, t)
-            remote(po.at[i, k2], pin.at[i, k], po_send.at[i], pin_recv.at[i], dev).start()
-            remote(st.at[i, k2], sin.at[i, k], st_send.at[i], sin_recv.at[i], dev).start()
-
-    def combine(c, i):
-        await_bytes(pin.at[i, pl.ds(0, 3)], pin_recv.at[i])
-        await_bytes(sin.at[i, pl.ds(0, 3)], sin_recv.at[i])
-        stats = [sin[i, n] for n in range(NK)]
-        top = jnp.maximum(jnp.maximum(stats[0], stats[1]), jnp.maximum(stats[2], stats[3]))
-        factor = [jnp.exp(s - top) for s in stats]
-        den = factor[0] * pltpu.roll(stats[0], 124, 1)
-        for n in range(1, NK):
-            den = den + factor[n] * pltpu.roll(stats[n], 124, 1)
-        weight = [f / den for f in factor]
-        for h in range(4):
-            cut = slice(h * HD, (h + 1) * HD)
-            num = weight[0][:, h:h + 1] * pin[i, 0, :, cut].astype(F32)
-            for n in range(1, NK):
-                num = num + weight[n][:, h:h + 1] * pin[i, n, :, cut].astype(F32)
-            att[i, :, cut] = num.astype(BF)
-        reach(att.at[i], ain.at[c_own, i, k], at_send.at[i], at_recv.at[i], (2 * k + c_own, d, t), spread_self)
-
-    def spread(c, i):
-        await_bytes(att.at[i], at_recv.at[i])
-        for n in range(1, NK):
-            dev = (((zh + n) % NK) * 2 + co, p, t)
-            remote(ain.at[co, i, zh], ain.at[co, i, zh], sp_send.at[i], sp_recv.at[i], dev).start()
+            o = o + jnp.dot(e[n].astype(BF), kvh[i, 1, n], preferred_element_type=F32)
+        att[i] = (o / den).astype(BF)
+        for n in range(NK):
+            dev = ((zh + n) % NK * 2 + k // 2, d, t)
+            reach(
+                att.at[i], ain.at[c_own, i, k], at_send.at[i], at_recv.at[c_own, i], dev,
+                query_self & ((zh + n) % NK == zh),
+            )
 
     def hand_over(c, i):
-        await_bytes(ain.at[co, i, pl.ds(0, 3)], sp_recv.at[i])
-        remote(ain.at[co, i], ain.at[co, i], fw_send.at[i], fw_recv.at[i], (sibling, p, t)).start()
+        pair = ain.at[c, i, pl.ds(2 * co, 2)]
+        await_bytes(pair, at_recv.at[c, i])
+        remote(pair, pair, fw_send.at[c, i], fw_recv.at[c, i], (sibling, p, t)).start()
 
     def mix(c, i):
         @pl.when((c == 0) & (i == 0))
         def _():
             loads[4].wait()
 
-        @pl.when(co != c)
-        def _():
-            await_bytes(ain.at[c, i], fw_recv.at[i])
-
-        pm[c, i] = jnp.dot(ain[c, i].reshape(64, 512), wo[...], preferred_element_type=F32)
+        await_bytes(ain.at[c, i, pl.ds(0, 2)], fw_recv.at[c, i])
+        rows = jnp.concatenate([ain[c, i, h] for h in range(NK)], axis=1)
+        pm[c, i] = jnp.dot(rows, wo[...], preferred_element_type=F32)
 
     def pass_on(c, slot, later, tensor_to, incoming):
         mine = pm[c, slot]
@@ -259,8 +239,7 @@
             out[c * 64:(c + 1) * 64] = (pm[c, 0] + rin[c, 0].astype(F32) + rin[c, 7].astype(F32)).astype(BF)
 
     stages = (
-        (project, None), (join_cores, None), (total_query, c_own), (attend, c_own), (combine, c_own),
-        (spread, co), (hand_over, co), (mix, None),
+        (project, None), (join_cores, None), (attend, c_own), (hand_over, None), (mix, None),
     )
 
     def step(u, carry):
@@ -321,16 +300,18 @@
             def _():
                 await_bytes(cnt.at[pl.ds(0, 2)], cnt_send.at[c])
 
-        await_bytes(qfull.at[i, pl.ds(0, 3)], xa_send.at[i])
-        await_bytes(po.at[i, pl.ds(0, 3)], po_send.at[i])
-        await_bytes(st.at[i, pl.ds(0, 3)], st_send.at[i])
-
-        @pl.when(jnp.logical_not(spread_self))
-        def _():
-            await_bytes(att.at[i], at_send.at[i])
-
-        await_bytes(ain.at[0, i, pl.ds(0, 3)], sp_send.at[i])
-        await_bytes(ain.at[0, i], fw_send.at[i])
+        await_bytes(kvh.at[i, :, pl.ds(0, 3)], kv_send.at[i])
+
+        @pl.when(query_self)
+        def _():
+            await_bytes(qin.at[i, pl.ds(0, 3)], at_send.at[i])
+
+        @pl.when(jnp.logical_not(query_self))
+        def _():
+            await_bytes(qin.at[i], at_send.at[i])
+
+        for c in range(2):
+            await_bytes(ain.at[c, i, pl.ds(0, 2)], fw_send.at[c, i])
         return carry
 
     lax.fori_loop(0, NG, drain, 0)
@@ -350,27 +331,22 @@
             pltpu.VMEM((NG, 2, 64, 1024), BF),
             pltpu.VMEM((1024, 512), BF),
             pltpu.VMEM((NG, 2, 128, 512), BF),
+            pltpu.VMEM((NG, 2, NK, 128, HD), BF),
             pltpu.VMEM((512, 1024), BF),
-            pltpu.VMEM((2, NG, NK, ROWS, 512), BF),
-            pltpu.VMEM((2, NG, 2, ROWS, 512), BF),
-            pltpu.VMEM((2, NG, 2, ROWS, 512), BF),
-            pltpu.VMEM((NG, NK, ROWS, 512), BF),
-            pltpu.VMEM((NG, NK, ROWS, 512), BF),
-            pltpu.VMEM((NG, NK, ROWS, 512), BF),
-            pltpu.VMEM((NG, NK, ROWS, 128), F32),
-            pltpu.VMEM((NG, NK, ROWS, 512), BF),
-            pltpu.VMEM((NG, NK, ROWS, 128), F32),
-            pltpu.VMEM((NG, ROWS, 512), BF),
-            pltpu.VMEM((2, NG, NK, ROWS, 512), BF),
+            pltpu.VMEM((2, NG, NK, 64, HD), BF),
+            pltpu.VMEM((2, NG, 2, 64, HD), BF),
+            pltpu.VMEM((2, NG, 2, 64, HD), BF),
+            pltpu.VMEM((NG, NK, 64, HD), BF),
+            pltpu.VMEM((NG, 64, HD), BF),
+            pltpu.VMEM((2, NG, NK, 64, HD), BF),
             pltpu.VMEM((2, NG, 64, 1024), F32),
             pltpu.VMEM((2, NG, 64, 1024), BF),
             pltpu.VMEM((2, NG, 64, 1024), BF),
             pltpu.VMEM((2, 2, 8, 128), jnp.int32),
             pltpu.VMEM((NK, 2, 8, 128), jnp.int32),
             dma((5,)), dma((2, 2)), dma((NG, 2)), dma((NG, 2)),
-            both, both, both, one, one, one,
-            one, one, one, one, one, one, one, one, one, one,
-            both, both, dma((2,)), dma((2,)), dma((2,)), dma((1,)),
+            both, both, both, one, one, one, one,
+            one, both, both, both, both, both, dma((2,)), dma((2,)), dma((2,)), dma((1,)),
         ],
         compiler_params=pltpu.CompilerParams(
             collective_id=0, has_side_effects=True, vmem_limit_bytes=60 * 1024 * 1024

time: 113 us -> 109 us (0.965)
  the two profiles are of different devices: /device:TPU:1 before, /device:TPU:6 now
where the time goes in v3:
time: 109 us; the launch traced here: 107 us
  Pallas kernels  106 us (97%)
  local copies, waits for them, and re-layouts  1.67 us (2%)
    pallas_call x1, Pallas kernels, on_device(): pl.pallas_call(kernel, out_shape=jax.ShapeDtypeStruct((128, 1024), BF), i...  106 us

profile of v3, /device:TPU:6, one launch (start us, length us, event | category | flops | bytes accessed | tf_op | source)
XLA Modules:
  0.0 107.2 jit_solution(11524410194239180705)
XLA Ops:
  0.0 105.6 %shard_map.55 = bf16[128,1024]{1,0:T(8,128)(2,1)} custom-call(bf16[2,64,1024]{2,1,0:T(8,128)(2,1)} %bitcast.9, bf16[1024,512]{1,0:T(8,128)(2,1)} %bitcast.7, bf16[8,2,128,512]{3,2,1,0:T(8,128)(2,1)} %bitcast.6, s32[1,1,2]{2,1,0:T(1,128)} %counts.1, bf16[512,1024]{1,0:T(8,128)(2,1)} %bitcast.8), custom_call_target="tpu_custom_call" | custom-call | flops 2500000000 | bytes 5000000 | tf_op jit(solution)/shard_map/pallas_call | solution.py:325
  105.6 1.7 %copy.7 = bf16[1,128,1024]{2,1,0:T(8,128)(2,1)} copy(bf16[1,128,1024]{2,1,0:T(8,128)(2,1)} %bitcast.5) | data formatting | bytes 524288

commit v4 on v3

--- a/solution.py
+++ b/solution.py
@@ -15,15 +15,17 @@
 NG = 8
 NK = 4
 UNITS = 2 * NG
-LAGS = (0, 2, 5, 8, 10)
+LAGS = (0, 2, 2, 6, 9, 11)
 BY_SPAN = False
+AHEAD = 2
+FIRST = 1
 RING_AT = {}
 
 
 def kernel(
     normed, wq_in, kv_in, counts, wo_in, out,
-    xg, wq, kv, kvh, wo, qp, sib, qs, qin, att, ain, pm, rsb, rin, cnt_two, cnt,
-    ld_sem, own_send, ag_send, ag_recv, sib_send, sib_recv, qs_send, qin_recv, kv_own, kv_send, kv_recv,
+    xg, wq, kv, kvh, via, wo, qp, sib, qs, qin, att, ain, pm, rsb, rin, cnt_two, cnt,
+    ld_sem, own_send, ag_send, ag_recv, sib_send, sib_recv, qs_send, qin_recv, kv_own, kv_send, kv_recv, via_send, via_recv, on_send,
     at_send, at_recv, fw_send, fw_recv, rs_send, rs_recv, c2_send, c2_recv, cnt_send, cnt_recv,
 ):
     d = lax.axis_index("dp")
@@ -63,9 +65,8 @@
         local(normed.at[0], xg.at[0, 0], ld_sem.at[0]),
         local(normed.at[1], xg.at[0, 1], ld_sem.at[1]),
         local(wq_in, wq, ld_sem.at[2]),
-        local(kv_in, kv, ld_sem.at[3]),
-        local(wo_in, wo, ld_sem.at[4]),
-    ]
+        local(wo_in, wo, ld_sem.at[3]),
+    ] + [local(kv_in.at[:, :, :, pl.ds(h * HD, HD)], kv.at[h], ld_sem.at[4 + h]) for h in range(NK)]
     for load in loads:
         load.start()
 
@@ -101,27 +102,34 @@
         remote(
             cnt_two.at[span, co], cnt_two.at[span, co], c2_send.at[span], c2_recv.at[span], (sibling, p, t)
         ).start()
-    loads[3].wait()
+    for h in range(NK):
+        loads[4 + h].wait()
 
     def sequence_of(i):
         hop = (i + 1) // 2
         return (t + NG + jnp.where(i % 2 == 1, -hop, hop)) % NG
 
-    def head_of(n):
-        return pl.ds(pl.multiple_of(n * HD, HD), HD)
+    def along_x(n):
+        return (d, c_own * NK + (k + n) % NK, t)
 
     def send_heads(i, carry):
         g = sequence_of(i)
-        local(kv.at[g, :, :, head_of(k)], kvh.at[i, :, k], kv_own.at[i]).start()
-        for n in range(1, NK):
-            k2 = (k + n) % NK
-            remote(
-                kv.at[g, :, :, head_of(k2)], kvh.at[i, :, k], kv_send.at[i], kv_recv.at[i],
-                (d, c_own * NK + k2, t),
-            ).start()
+        local(kv.at[k, g], kvh.at[i, k], kv_own.at[i]).start()
+        for n in (1, 3):
+            remote(kv.at[(k + n) % NK, g], kvh.at[i, k], kv_send.at[i], kv_recv.at[i], along_x(n)).start()
+        far = kv.at[(k + 2) % NK, g]
+
+        @pl.when(i % 2 == 0)
+        def _():
+            remote(far, kvh.at[i, k], kv_send.at[i], kv_recv.at[i], along_x(2)).start()
+
+        @pl.when(i % 2 == 1)
+        def _():
+            remote(far, via.at[i // 2], via_send.at[i // 2], via_recv.at[i // 2], along_x(FIRST)).start()
+
         return carry
 
-    lax.fori_loop(0, NG, send_heads, 0)
+    lax.fori_loop(0, AHEAD, send_heads, 0)
     loads[2].wait()
 
     def project(c, i):
@@ -135,6 +143,10 @@
             @pl.when((i <= 4) | (i == 5 + c))
             def _():
                 remote(xg.at[i, c], xg.at[later, c], ag_send.at[i, c], ag_recv.at[later, c], target).start()
+
+        @pl.when((c == 0) & (i < NG - AHEAD))
+        def _():
+            send_heads(i + AHEAD, 0)
 
         part = jnp.dot(xg[i, c], wq[...], preferred_element_type=F32).astype(BF)
         for h in range(NK):
@@ -157,13 +169,20 @@
             qs[c, i, n] = (qp[c, i, 2 * co + n].astype(F32) + sib[c, i, n].astype(F32)).astype(BF)
             reach(qs.at[c, i, n], qin.at[i, zh], qs_send.at[c, i], qin_recv.at[i], (p, b, t), on_diag & (b == p))
 
+    def relay(c, i):
+        @pl.when(i % 2 == 1)
+        def _():
+            j = i // 2
+            await_bytes(via.at[j], via_recv.at[j])
+            remote(via.at[j], kvh.at[i, (k + NK - FIRST) % NK], on_send.at[j], kv_recv.at[i], along_x(FIRST)).start()
+
     def attend(c, i):
         @pl.when(i == 0)
         def _():
             await_bytes(cnt, cnt_recv.at[0])
 
-        await_bytes(kvh.at[i, :, 0], kv_own.at[i])
-        await_bytes(kvh.at[i, :, pl.ds(0, 3)], kv_recv.at[i])
+        await_bytes(kvh.at[i, 0], kv_own.at[i])
+        await_bytes(kvh.at[i, pl.ds(0, 3)], kv_recv.at[i])
         await_bytes(qin.at[i], qin_recv.at[i])
         total = qin[i, 0].astype(F32)
         for n in range(1, NK):
@@ -174,7 +193,7 @@
         scores = []
         for n in range(NK):
             s = lax.dot_general(
-                q, kvh[i, 0, n], (((1,), (1,)), ((), ())), preferred_element_type=F32
+                q, kvh[i, n, 0], (((1,), (1,)), ((), ())), preferred_element_type=F32
             ) * (1.0 / math.sqrt(HD))
             scores.append(jnp.where(count > n, s, NEG))
         top = jnp.max(
@@ -182,9 +201,9 @@
         )
         e = [jnp.exp(s - top) for s in scores]
         den = jnp.sum((e[0] + e[1]) + (e[2] + e[3]), axis=1, keepdims=True)
-        o = jnp.dot(e[0].astype(BF), kvh[i, 1, 0], preferred_element_type=F32)
+        o = jnp.dot(e[0].astype(BF), kvh[i, 0, 1], preferred_element_type=F32)
         for n in range(1, NK):
-            o = o + jnp.dot(e[n].astype(BF), kvh[i, 1, n], preferred_element_type=F32)
+            o = o + jnp.dot(e[n].astype(BF), kvh[i, n, 1], preferred_element_type=F32)
         att[i] = (o / den).astype(BF)
         for n in range(NK):
             dev = ((zh + n) % NK * 2 + k // 2, d, t)
@@ -201,7 +220,7 @@
     def mix(c, i):
         @pl.when((c == 0) & (i == 0))
         def _():
-            loads[4].wait()
+            loads[3].wait()
 
         await_bytes(ain.at[c, i, pl.ds(0, 2)], fw_recv.at[c, i])
         rows = jnp.concatenate([ain[c, i, h] for h in range(NK)], axis=1)
@@ -239,7 +258,7 @@
             out[c * 64:(c + 1) * 64] = (pm[c, 0] + rin[c, 0].astype(F32) + rin[c, 7].astype(F32)).astype(BF)
 
     stages = (
-        (project, None), (join_cores, None), (attend, c_own), (hand_over, None), (mix, None),
+        (project, None), (join_cores, None), (relay, c_own), (attend, c_own), (hand_over, None), (mix, None),
     )
 
     def step(u, carry):
@@ -300,7 +319,17 @@
             def _():
                 await_bytes(cnt.at[pl.ds(0, 2)], cnt_send.at[c])
 
-        await_bytes(kvh.at[i, :, pl.ds(0, 3)], kv_send.at[i])
+
+        @pl.when(i % 2 == 0)
+        def _():
+            await_bytes(kvh.at[i, pl.ds(0, 3)], kv_send.at[i])
+
+        @pl.when(i % 2 == 1)
+        def _():
+            await_bytes(kvh.at[i, pl.ds(0, 2)], kv_send.at[i])
+            await_bytes(via.at[i // 2], via_send.at[i // 2])
+            await_bytes(via.at[i // 2], on_send.at[i // 2])
+
 
         @pl.when(query_self)
         def _():
@@ -330,8 +359,9 @@
         scratch_shapes=[
             pltpu.VMEM((NG, 2, 64, 1024), BF),
             pltpu.VMEM((1024, 512), BF),
-            pltpu.VMEM((NG, 2, 128, 512), BF),
-            pltpu.VMEM((NG, 2, NK, 128, HD), BF),
+            pltpu.VMEM((NK, NG, 2, 128, HD), BF),
+            pltpu.VMEM((NG, NK, 2, 128, HD), BF),
+            pltpu.VMEM((NG // 2, 2, 128, HD), BF),
             pltpu.VMEM((512, 1024), BF),
             pltpu.VMEM((2, NG, NK, 64, HD), BF),
             pltpu.VMEM((2, NG, 2, 64, HD), BF),
@@ -344,9 +374,9 @@
             pltpu.VMEM((2, NG, 64, 1024), BF),
             pltpu.VMEM((2, 2, 8, 128), jnp.int32),
             pltpu.VMEM((NK, 2, 8, 128), jnp.int32),
-            dma((5,)), dma((2, 2)), dma((NG, 2)), dma((NG, 2)),
+            dma((8,)), dma((2, 2)), dma((NG, 2)), dma((NG, 2)),
             both, both, both, one, one, one, one,
-            one, both, both, both, both, both, dma((2,)), dma((2,)), dma((2,)), dma((1,)),
+            dma((NG // 2,)), dma((NG // 2,)), dma((NG // 2,)), one, both, both, both, both, both, dma((2,)), dma((2,)), dma((2,)), dma((1,)),
         ],
         compiler_params=pltpu.CompilerParams(
             collective_id=0, has_side_effects=True, vmem_limit_bytes=60 * 1024 * 1024

time: 109 us -> 99.3 us (0.911)
  Pallas kernels: 106 us -> 95.8 us
    pallas_call x1, Pallas kernels: 106 us -> 95.8 us  [on_device(): pl.pallas_call(kernel, out_shape=jax.ShapeDtypeStruct((128, 1024), BF), i...]
where the time goes in v4:
time: 99.3 us; the launch traced here: 97.5 us
  Pallas kernels  95.8 us (96%)
  local copies, waits for them, and re-layouts  1.67 us (2%)
    pallas_call x1, Pallas kernels, on_device(): pl.pallas_call(kernel, out_shape=jax.ShapeDtypeStruct((128, 1024), BF), i...  95.8 us

profile of v4, /device:TPU:6, one launch (start us, length us, event | category | flops | bytes accessed | tf_op | source)
XLA Modules:
  0.0 97.5 jit_solution(15203111893568255489)
XLA Ops:
  0.0 95.8 %shard_map.55 = bf16[128,1024]{1,0:T(8,128)(2,1)} custom-call(bf16[2,64,1024]{2,1,0:T(8,128)(2,1)} %bitcast.9, bf16[1024,512]{1,0:T(8,128)(2,1)} %bitcast.7, bf16[8,2,128,512]{3,2,1,0:T(8,128)(2,1)} %bitcast.6, s32[1,1,2]{2,1,0:T(1,128)} %counts.1, bf16[512,1024]{1,0:T(8,128)(2,1)} %bitcast.8), custom_call_target="tpu_custom_call" | custom-call | flops 2500000000 | bytes 5000000 | tf_op jit(solution)/shard_map/pallas_call | solution.py:354
  95.8 1.7 %copy.7 = bf16[1,128,1024]{2,1,0:T(8,128)(2,1)} copy(bf16[1,128,1024]{2,1,0:T(8,128)(2,1)} %bitcast.5) | data formatting | bytes 524288

commit v5 on v4

--- a/solution.py
+++ b/solution.py
@@ -17,6 +17,8 @@
 UNITS = 2 * NG
 LAGS = (0, 2, 2, 6, 9, 11)
 BY_SPAN = False
+STAG_AG = True
+STAG_RS = True
 AHEAD = 2
 FIRST = 1
 RING_AT = {}
@@ -94,10 +96,14 @@
         cnt_two[span, co] = jnp.full((8, 128), counts[0, 0, span], jnp.int32)
     pl.semaphore_wait(barrier, 14 - 2 * jnp.where(query_self, 1, 0))
 
-    for half in range(2):
+    def send_own(half):
         loads[half].wait()
         remote(xg.at[0, half], xg.at[1, half], own_send.at[0, half], ag_recv.at[1, half], (d, p, up)).start()
         remote(xg.at[0, half], xg.at[2, half], own_send.at[1, half], ag_recv.at[2, half], (d, p, dn)).start()
+
+    send_own(0)
+    if not STAG_AG:
+        send_own(1)
     for span in range(2):
         remote(
             cnt_two.at[span, co], cnt_two.at[span, co], c2_send.at[span], c2_recv.at[span], (sibling, p, t)
@@ -130,6 +136,10 @@
         return carry
 
     lax.fori_loop(0, AHEAD, send_heads, 0)
+    if STAG_AG:
+        for way in range(2):
+            await_bytes(xg.at[0, 0], own_send.at[way, 0])
+        send_own(1)
     loads[2].wait()
 
     def project(c, i):
@@ -242,6 +252,9 @@
         if r == 0 and c == 0:
             pass_on(c, 7, 5, dn, False)
             pass_on(c, 6, 4, up, False)
+            if STAG_RS:
+                for slot in (7, 6):
+                    await_bytes(rsb.at[c, slot], rs_send.at[c, slot])
         elif r == 0:
             pass_on(c, 7, 6, up, False)
             pass_on(c, 5, 3, dn, False)
@@ -285,7 +298,7 @@
                 ring(c, r)
 
     for way in range(2):
-        for half in range(2):
+        for half in range(1 if STAG_AG else 0, 2):
             await_bytes(xg.at[0, half], own_send.at[way, half])
     for i in range(1, 7):
         for half in range(2):
@@ -296,7 +309,7 @@
 
     def drain(i, carry):
         for c in range(2):
-            @pl.when(i >= 1)
+            @pl.when((i >= 1) & (i < 6) if STAG_RS and c == 0 else (i >= 1))
             def _():
                 await_bytes(rsb.at[c, i], rs_send.at[c, i])
 

time: 99.3 us -> 98.8 us (level)
  no operation moved by 1% of the time
where the time goes in v5:
time: 98.8 us; the launch traced here: 97.9 us
  Pallas kernels  96.2 us (97%)
  local copies, waits for them, and re-layouts  1.67 us (2%)
    pallas_call x1, Pallas kernels, on_device(): pl.pallas_call(kernel, out_shape=jax.ShapeDtypeStruct((128, 1024), BF), i...  96.2 us

profile of v5, /device:TPU:6, one launch (start us, length us, event | category | flops | bytes accessed | tf_op | source)
XLA Modules:
  0.0 97.9 jit_solution(12709169339609828943)
XLA Ops:
  0.0 96.2 %shard_map.55 = bf16[128,1024]{1,0:T(8,128)(2,1)} custom-call(bf16[2,64,1024]{2,1,0:T(8,128)(2,1)} %bitcast.9, bf16[1024,512]{1,0:T(8,128)(2,1)} %bitcast.7, bf16[8,2,128,512]{3,2,1,0:T(8,128)(2,1)} %bitcast.6, s32[1,1,2]{2,1,0:T(1,128)} %counts.1, bf16[512,1024]{1,0:T(8,128)(2,1)} %bitcast.8), custom_call_target="tpu_custom_call" | custom-call | flops 2500000000 | bytes 5000000 | tf_op jit(solution)/shard_map/pallas_call | solution.py:367
  96.2 1.7 %copy.7 = bf16[1,128,1024]{2,1,0:T(8,128)(2,1)} copy(bf16[1,128,1024]{2,1,0:T(8,128)(2,1)} %bitcast.5) | data formatting | bytes 524288

commit v6 on v5

--- a/solution.py
+++ b/solution.py
@@ -15,19 +15,18 @@
 NG = 8
 NK = 4
 UNITS = 2 * NG
-LAGS = (0, 2, 2, 6, 9, 11)
+LAGS = (0, 2, 6, 9, 11)
 BY_SPAN = False
 STAG_AG = True
 STAG_RS = True
 AHEAD = 2
-FIRST = 1
 RING_AT = {}
 
 
 def kernel(
     normed, wq_in, kv_in, counts, wo_in, out,
-    xg, wq, kv, kvh, via, wo, qp, sib, qs, qin, att, ain, pm, rsb, rin, cnt_two, cnt,
-    ld_sem, own_send, ag_send, ag_recv, sib_send, sib_recv, qs_send, qin_recv, kv_own, kv_send, kv_recv, via_send, via_recv, on_send,
+    xg, wq, kv, kvh, wo, qp, sib, qs, qin, att, ain, pm, rsb, rin, cnt_two, cnt,
+    ld_sem, own_send, ag_send, ag_recv, sib_send, sib_recv, qs_send, qin_recv, kv_own, kv_send, kv_recv,
     at_send, at_recv, fw_send, fw_recv, rs_send, rs_recv, c2_send, c2_recv, cnt_send, cnt_recv,
 ):
     d = lax.axis_index("dp")
@@ -82,8 +81,6 @@
         def _():
             greet(dev)
 
-    greet((d, p, up))
-    greet((d, p, dn))
     for n in range(NK):
         b = (n % 2) * NK + 2 * co + n // 2
         greet_other((p, b, t), on_diag & (b == p))
@@ -91,6 +88,8 @@
         greet_other((source, d, t), on_diag & (source == d))
     for n in range(1, NK):
         greet((d, c_own * NK + (k + n) % NK, t))
+    greet((d, p, up))
+    greet((d, p, dn))
     greet((sibling, p, t))
     for span in range(2):
         cnt_two[span, co] = jnp.full((8, 128), counts[0, 0, span], jnp.int32)
@@ -121,18 +120,8 @@
     def send_heads(i, carry):
         g = sequence_of(i)
         local(kv.at[k, g], kvh.at[i, k], kv_own.at[i]).start()
-        for n in (1, 3):
+        for n in (1, 3, 2):
             remote(kv.at[(k + n) % NK, g], kvh.at[i, k], kv_send.at[i], kv_recv.at[i], along_x(n)).start()
-        far = kv.at[(k + 2) % NK, g]
-
-        @pl.when(i % 2 == 0)
-        def _():
-            remote(far, kvh.at[i, k], kv_send.at[i], kv_recv.at[i], along_x(2)).start()
-
-        @pl.when(i % 2 == 1)
-        def _():
-            remote(far, via.at[i // 2], via_send.at[i // 2], via_recv.at[i // 2], along_x(FIRST)).start()
-
         return carry
 
     lax.fori_loop(0, AHEAD, send_heads, 0)
@@ -178,13 +167,6 @@
             b = c * NK + 2 * co + n
             qs[c, i, n] = (qp[c, i, 2 * co + n].astype(F32) + sib[c, i, n].astype(F32)).astype(BF)
             reach(qs.at[c, i, n], qin.at[i, zh], qs_send.at[c, i], qin_recv.at[i], (p, b, t), on_diag & (b == p))
-
-    def relay(c, i):
-        @pl.when(i % 2 == 1)
-        def _():
-            j = i // 2
-            await_bytes(via.at[j], via_recv.at[j])
-            remote(via.at[j], kvh.at[i, (k + NK - FIRST) % NK], on_send.at[j], kv_recv.at[i], along_x(FIRST)).start()
 
     def attend(c, i):
         @pl.when(i == 0)
@@ -271,7 +253,7 @@
             out[c * 64:(c + 1) * 64] = (pm[c, 0] + rin[c, 0].astype(F32) + rin[c, 7].astype(F32)).astype(BF)
 
     stages = (
-        (project, None), (join_cores, None), (relay, c_own), (attend, c_own), (hand_over, None), (mix, None),
+        (project, None), (join_cores, None), (attend, c_own), (hand_over, None), (mix, None),
     )
 
     def step(u, carry):
@@ -332,17 +314,7 @@
             def _():
                 await_bytes(cnt.at[pl.ds(0, 2)], cnt_send.at[c])
 
-
-        @pl.when(i % 2 == 0)
-        def _():
-            await_bytes(kvh.at[i, pl.ds(0, 3)], kv_send.at[i])
-
-        @pl.when(i % 2 == 1)
-        def _():
-            await_bytes(kvh.at[i, pl.ds(0, 2)], kv_send.at[i])
-            await_bytes(via.at[i // 2], via_send.at[i // 2])
-            await_bytes(via.at[i // 2], on_send.at[i // 2])
-
+        await_bytes(kvh.at[i, pl.ds(0, 3)], kv_send.at[i])
 
         @pl.when(query_self)
         def _():
@@ -374,7 +346,6 @@
             pltpu.VMEM((1024, 512), BF),
             pltpu.VMEM((NK, NG, 2, 128, HD), BF),
             pltpu.VMEM((NG, NK, 2, 128, HD), BF),
-            pltpu.VMEM((NG // 2, 2, 128, HD), BF),
             pltpu.VMEM((512, 1024), BF),
             pltpu.VMEM((2, NG, NK, 64, HD), BF),
             pltpu.VMEM((2, NG, 2, 64, HD), BF),
@@ -389,7 +360,7 @@
             pltpu.VMEM((NK, 2, 8, 128), jnp.int32),
             dma((8,)), dma((2, 2)), dma((NG, 2)), dma((NG, 2)),
             both, both, both, one, one, one, one,
-            dma((NG // 2,)), dma((NG // 2,)), dma((NG // 2,)), one, both, both, both, both, both, dma((2,)), dma((2,)), dma((2,)), dma((1,)),
+            one, both, both, both, both, both, dma((2,)), dma((2,)), dma((2,)), dma((1,)),
         ],
         compiler_params=pltpu.CompilerParams(
             collective_id=0, has_side_effects=True, vmem_limit_bytes=60 * 1024 * 1024

time: 98.8 us -> 95.5 us (0.967)
  Pallas kernels: 96.2 us -> 93.4 us
    pallas_call x1, Pallas kernels: 96.2 us -> 93.4 us  [on_device(): pl.pallas_call(kernel, out_shape=jax.ShapeDtypeStruct((128, 1024), BF), i...]
where the time goes in v6:
time: 95.5 us; the launch traced here: 95.1 us
  Pallas kernels  93.4 us (98%)
  local copies, waits for them, and re-layouts  1.67 us (2%)
    pallas_call x1, Pallas kernels, on_device(): pl.pallas_call(kernel, out_shape=jax.ShapeDtypeStruct((128, 1024), BF), i...  93.4 us

profile of v6, /device:TPU:6, one launch (start us, length us, event | category | flops | bytes accessed | tf_op | source)
XLA Modules:
  0.0 95.1 jit_solution(12656615204122644186)
XLA Ops:
  0.0 93.4 %shard_map.55 = bf16[128,1024]{1,0:T(8,128)(2,1)} custom-call(bf16[2,64,1024]{2,1,0:T(8,128)(2,1)} %bitcast.9, bf16[1024,512]{1,0:T(8,128)(2,1)} %bitcast.7, bf16[8,2,128,512]{3,2,1,0:T(8,128)(2,1)} %bitcast.6, s32[1,1,2]{2,1,0:T(1,128)} %counts.1, bf16[512,1024]{1,0:T(8,128)(2,1)} %bitcast.8), custom_call_target="tpu_custom_call" | custom-call | flops 2500000000 | bytes 5000000 | tf_op jit(solution)/shard_map/pallas_call | solution.py:339
  93.4 1.7 %copy.7 = bf16[1,128,1024]{2,1,0:T(8,128)(2,1)} copy(bf16[1,128,1024]{2,1,0:T(8,128)(2,1)} %bitcast.5) | data formatting | bytes 524288

commit v7 on v6

--- a/solution.py
+++ b/solution.py
@@ -15,7 +15,7 @@
 NG = 8
 NK = 4
 UNITS = 2 * NG
-LAGS = (0, 2, 6, 9, 11)
+LAGS = (0, 2, 6, 10, 12)
 BY_SPAN = False
 STAG_AG = True
 STAG_RS = True

time: 95.5 us -> 95.8 us (level)
  no operation moved by 1% of the time
where the time goes in v7:
time: 95.8 us; the launch traced here: 95.4 us
  Pallas kernels  93.8 us (98%)
  local copies, waits for them, and re-layouts  1.67 us (2%)
    pallas_call x1, Pallas kernels, on_device(): pl.pallas_call(kernel, out_shape=jax.ShapeDtypeStruct((128, 1024), BF), i...  93.8 us

profile of v7, /device:TPU:6, one launch (start us, length us, event | category | flops | bytes accessed | tf_op | source)
XLA Modules:
  0.0 95.4 jit_solution(4661114630531489182)
XLA Ops:
  0.0 93.8 %shard_map.55 = bf16[128,1024]{1,0:T(8,128)(2,1)} custom-call(bf16[2,64,1024]{2,1,0:T(8,128)(2,1)} %bitcast.9, bf16[1024,512]{1,0:T(8,128)(2,1)} %bitcast.7, bf16[8,2,128,512]{3,2,1,0:T(8,128)(2,1)} %bitcast.6, s32[1,1,2]{2,1,0:T(1,128)} %counts.1, bf16[512,1024]{1,0:T(8,128)(2,1)} %bitcast.8), custom_call_target="tpu_custom_call" | custom-call | flops 2500000000 | bytes 5000000 | tf_op jit(solution)/shard_map/pallas_call | solution.py:339
  93.8 1.7 %copy.7 = bf16[1,128,1024]{2,1,0:T(8,128)(2,1)} copy(bf16[1,128,1024]{2,1,0:T(8,128)(2,1)} %bitcast.5) | data formatting | bytes 524288
